TPU v7x, 32 devices: a whole 2x2x4 slice. The times are simulated.
32 devices in a mesh: ctx: 8 (over z, y), tp: 4 (over x, core).
Axes of the slice: x: 2, y: 2, z: 4, core: 2. Of those that a mesh axis runs over, the one named last changes fastest.
Arguments:
- query_proj: bfloat16 [2048, 8192], P('ctx', 'tp'), may hold values from -24 to 24, as said below
- key_proj: bfloat16 [2048, 8192], P('ctx', 'tp'), may hold values from -6 to 6
- value_proj: bfloat16 [2048, 8192], P('ctx', 'tp'), may hold values from -6 to 6
- filters: bfloat16 [128, 8192], P(None, 'tp'), may hold values from -6 to 6, as said below
- norm_gain: float32 [8192], P('tp'), may hold values from 0.1 to 1.9
- grad_out: bfloat16 [2048, 8192], P('ctx', 'tp'), may hold values from -6 to 6
Outputs:
- mixed: bfloat16 [2048, 8192], P('ctx', 'tp')
- grad_query: bfloat16 [2048, 8192], P('ctx', 'tp')
- grad_key: bfloat16 [2048, 8192], P('ctx', 'tp')
- grad_value: bfloat16 [2048, 8192], P('ctx', 'tp')
- grad_filter: float32 [128, 8192], P(None, 'tp')
- grad_gain: float32 [8192], P('tp')
Inputs may be any that keep to these rules, and one draw needn't show every extreme that they name: `query_proj`: finite real values. `filters`: finite real values.
All inputs are finite; a program needn't handle non-finite values.
Results may differ from a plain program's by a relative error of at most 0.0051.
Values may be sent and summed in bfloat16 or wider, within the bound.
A program may use at most 64 MiB of HBM per device.

v0:
```python
import math
import jax
import jax.numpy as jnp
import numpy as np
from jax import lax
from jax.sharding import PartitionSpec as P

EPS = 1e-06
F32 = jnp.float32
BF16 = jnp.bfloat16


def passed_along(array, axis, by):
    length = lax.axis_size(axis)
    pairs = [(i, i + by) for i in range(length) if 0 <= i + by < length]
    return lax.ppermute(array, axis, pairs)


def split(array):
    high = array.astype(BF16)
    return (high, (array - high.astype(array.dtype)).astype(BF16))


def dft_matrices(block):
    length = 2 * block
    freq = np.concatenate([np.arange(0, block, 2), np.arange(1, block, 2)])
    at = np.arange(block)
    angle = 2.0 * np.pi * (freq[:, None] * at[None, :] % length) / length
    sign = np.where(at % 2 == 0, 1.0, -1.0)
    real, imag = (np.cos(angle), -np.sin(angle))
    imag[0] = sign
    forward = np.concatenate([real, imag], 0)
    back = np.concatenate([2.0 * real, 2.0 * imag], 0)
    back[0] *= 0.5
    back[block] *= 0.5
    back = back.T / length

    def parts(matrix):
        matrix = matrix.astype(np.float32)
        high = matrix.astype(jnp.bfloat16)
        low = (matrix - high.astype(np.float32)).astype(jnp.bfloat16)
        return (high, low)

    fh, fl = parts(forward)
    bh, bl = parts(back)
    return (np.concatenate([fh, fl], 1), np.concatenate([bh, bl, bh], 1))


def flip(spec):
    quarter = spec.shape[0] // 4
    return jnp.concatenate(
        [
            spec[:quarter],
            -spec[quarter : 2 * quarter],
            spec[2 * quarter : 3 * quarter],
            -spec[3 * quarter :],
        ],
        0,
    )


def product(a, b, conj):
    half = a.shape[0] // 2
    ar, ai, br, bi = (a[:half], a[half:], b[:half], b[half:])
    first = lax.broadcasted_iota(jnp.int32, ar.shape, 0) == 0
    rr, ii = (ar * br, ai * bi)
    if conj:
        real = jnp.where(first, rr, rr + ii)
        imag = jnp.where(first, ii, ai * br - ar * bi)
    else:
        real = jnp.where(first, rr, rr - ii)
        imag = jnp.where(first, ii, ai * br + ar * bi)
    return jnp.concatenate([real, imag], 0)


def on_device(query_proj, key_proj, value_proj, filters, norm_gain, grad_out):
    row_count, col_count = query_proj.shape
    taps = filters.shape[0]
    blocks = row_count // taps
    width = col_count * lax.axis_size("tp")
    scale = 1.0 / math.sqrt(row_count * lax.axis_size("ctx"))
    forward, back = dft_matrices(taps)

    def to_spec(rows):
        return jnp.dot(forward, jnp.concatenate([rows, rows], 0), preferred_element_type=F32)

    def from_spec(spec):
        high, low = split(spec)
        return jnp.dot(back, jnp.concatenate([high, high, low], 0), preferred_element_type=F32)

    key_wide = key_proj.astype(F32)
    value_wide = value_proj.astype(F32)
    query_wide = query_proj.astype(F32)
    key_value = (key_wide * value_wide).astype(BF16)
    before = passed_along(key_value[row_count - taps :], "ctx", 1)
    filt = to_spec(filters)
    kv_spec = [to_spec(before)] + [
        to_spec(key_value[b * taps : (b + 1) * taps]) for b in range(blocks)
    ]
    kv_win = [kv_spec[b + 1] + flip(kv_spec[b]) for b in range(blocks)]
    conv_out = jnp.concatenate([from_spec(product(w, filt, False)) for w in kv_win], 0)
    gated = query_wide * conv_out
    grad_wide = grad_out.astype(F32)
    grad_scaled = grad_wide * norm_gain
    stats = lax.psum(jnp.stack([jnp.sum(gated * gated, 1), jnp.sum(grad_scaled * gated, 1)]), "tp")
    inv_rms = lax.rsqrt(stats[0] / width + EPS)
    row_mean = stats[1] * inv_rms / width
    normed = gated * inv_rms[:, None]
    mixed = (normed * norm_gain).astype(BF16)
    grad_gated = (grad_scaled - normed * row_mean[:, None]) * inv_rms[:, None]
    grad_query = (grad_gated * conv_out).astype(BF16)
    grad_conv = (grad_gated * query_wide).astype(BF16)
    after = passed_along(grad_conv[:taps], "ctx", -1)
    gc_spec = [to_spec(grad_conv[b * taps : (b + 1) * taps]) for b in range(blocks)]
    filter_spec = sum((product(gc_spec[b], kv_win[b], True) for b in range(blocks)))
    filter_local = from_spec(filter_spec)
    gain_local = jnp.sum(grad_wide * normed, 0)
    total = lax.psum(jnp.concatenate([filter_local, gain_local[None]], 0), "ctx") * scale
    gc_spec = gc_spec + [to_spec(after)]
    gc_win = [gc_spec[b] + flip(gc_spec[b + 1]) for b in range(blocks)]
    grad_kv = jnp.concatenate([from_spec(product(w, filt, True)) for w in gc_win], 0)
    grad_key = (grad_kv * value_wide).astype(BF16)
    grad_value = (grad_kv * key_wide).astype(BF16)
    return (mixed, grad_query, grad_key, grad_value, total[:taps], total[taps])


def solution(mesh):
    placed = (
        P("ctx", "tp"),
        P("ctx", "tp"),
        P("ctx", "tp"),
        P(None, "tp"),
        P("tp"),
        P("ctx", "tp"),
    )
    return jax.shard_map(
        on_device,
        mesh=mesh,
        in_specs=placed,
        out_specs=(
            P("ctx", "tp"),
            P("ctx", "tp"),
            P("ctx", "tp"),
            P("ctx", "tp"),
            P(None, "tp"),
            P("tp"),
        ),
        check_vma=False,
    )
```

profile of v0, /device:TPU:0, one launch (start us, length us, event | category | flops | bytes accessed | tf_op | source)
XLA Modules:
  0.0 159.9 jit_solution(13736018145283497802)
XLA Ops:
  7.2 2.0 %fusion.18 = bf16[256,2048]{1,0:T(8,128)(2,1)S(1)} fusion(bf16[256,2048]{1,0:T(8,128)(2,1)} %param.10, bf16[256,2048]{1,0:T(8,128)(2,1)} %param.9), kind=kLoop, calls=%fused_computation.42 | loop fusion | flops 2097152 | bytes 3145728 | tf_op jit(solution)/shard_map/convert_element_type | solution.py:94
  9.3 4.9 %collective-permute-start = (bf16[128,2048]{1,0:T(8,128)(2,1)S(1)}, bf16[128,2048]{1,0:T(8,128)(2,1)S(1)}, u32[]{:S(2)}, u32[]{:S(2)}) collective-permute-start(bf16[128,2048]{1,0:T(8,128)(2,1)S(1)} %slice.194), channel_id=1, source_target_pairs={{0,4},{4,8},{8,12},{12,16},{16,20},{20,24},{24,28},{1,5},{5,9},{9,... | collective-permute-start | bytes 1572872 | tf_op jit(solution)/shard_map/ppermute | solution.py:16
  14.2 0.4 fusion.67
  14.6 0.4 fusion.29
  15.1 0.4 fusion.74
  15.5 0.4 convolution_add_fusion.6
  16.0 9.4 %collective-permute-done = bf16[128,2048]{1,0:T(8,128)(2,1)S(1)} collective-permute-done((bf16[128,2048]{1,0:T(8,128)(2,1)S(1)}, bf16[128,2048]{1,0:T(8,128)(2,1)S(1)}, u32[]{:S(2)}, u32[]{:S(2)}) %collective-permute-start) | collective-permute-done | bytes 524320 | tf_op jit(solution)/shard_map/ppermute | solution.py:16
  25.3 0.4 fusion.75
  25.7 0.4 fusion.5
  26.3 0.7 maximum_add_fusion
  27.2 0.5 fusion.4
  27.7 1.0 subtract_select_fusion.1
  28.6 0.4 copy-done.2
  29.1 0.3 fusion.32
  29.4 0.5 copy-done.14
  29.9 0.3 convolution_add_fusion.16
  30.3 0.3 fusion.13
  31.3 0.3 fusion.12
  31.6 1.0 copy-done.6
  32.6 0.6 copy-done.11
  33.1 0.7 multiply_reduce_fusion
  33.8 5.7 %psum.14 = f32[2,256]{1,0:T(2,128)S(1)} all-reduce(f32[2,256]{1,0:T(2,128)S(1)} %pad_maximum_fusion.7), channel_id=1, replica_groups=mesh['ctx'=8,'tp'=4] {'tp'}, use_global_device_ids=true, to_apply=%region_2.3 | all-reduce | flops 512 | bytes 4096 | tf_op jit(solution)/shard_map/psum | solution.py:105
  39.6 4.5 %fusion.16 = (bf16[256,2048]{1,0:T(8,128)(2,1)S(1)}, bf16[256,2048]{1,0:T(8,128)(2,1)}, f32[2048]{0:T(1024)S(1)}, bf16[256,2048]{1,0:T(8,128)(2,1)}) fusion(bf16[256,2048]{1,0:T(8,128)(2,1)} %param.8, f32[256]{0:T(256)S(1)} %multiply_multiply_fusion, f32[256]{0:T(256)S(1)} %bitcast.69, f32[2048]{0:T(1024)S(1)} %copy-done.15, bf16[256,2048]{1,0:T(8,128)(2,1)} %param.13, ...), kind=kLoop, calls=%fused_computation.40 | loop fusion | flops 8910848 | bytes 7358464 | tf_op jit(solution)/shard_map/convert_element_type | solution.py:112
  44.1 1.5 collective-permute-start.1
  45.6 0.4 fusion.64
  46.1 0.4 fusion.26
  46.5 14.0 %collective-permute-done.1 = bf16[128,2048]{1,0:T(8,128)(2,1)S(1)} collective-permute-done((bf16[128,2048]{1,0:T(8,128)(2,1)S(1)}, bf16[128,2048]{1,0:T(8,128)(2,1)S(1)}, u32[]{:S(2)}, u32[]{:S(2)}) %collective-permute-start.1) | collective-permute-done | bytes 524320 | tf_op jit(solution)/shard_map/ppermute | solution.py:16
  60.4 0.4 fusion.76
  60.9 0.4 fusion
  61.5 1.8 %maximum_add_fusion.2 = (f32[256,2048]{1,0:T(8,128)}, f32[256,2048]{1,0:T(8,128)S(1)}) fusion(f32[64,2048]{1,0:T(8,128)S(1)} %get-tuple-element.35, f32[64,2048]{1,0:T(8,128)S(1)} %get-tuple-element.36, f32[64,2048]{1,0:T(8,128)S(1)} %get-tuple-element.37, f32[64,2048]{1,0:T(8,128)S(1)} %get-tuple-element.34, f32[2048,256]{0,1:T(8,128)S(1)} %fusion.26, ...), kind=kOutput, calls=%fused_computation.51 | convolution fusion | flops 136839168 | bytes 8978432 | tf_op jit(solution)/shard_map/dot_general | solution.py:85
  63.5 1.8 %maximum_add_fusion.1 = (f32[256,2048]{1,0:T(8,128)}, f32[256,2048]{1,0:T(8,128)S(1)}) fusion(f32[64,2048]{1,0:T(8,128)S(1)} %get-tuple-element.31, f32[64,2048]{1,0:T(8,128)S(1)} %get-tuple-element.32, f32[64,2048]{1,0:T(8,128)S(1)} %get-tuple-element.33, f32[64,2048]{1,0:T(8,128)S(1)} %get-tuple-element.30, f32[2048,256]{0,1:T(8,128)S(1)} %fusion.64, ...), kind=kOutput, calls=%fused_computation.49 | convolution fusion | flops 136839168 | bytes 8978432 | tf_op jit(solution)/shard_map/dot_general | solution.py:85
  65.4 1.2 add_select_fusion.1
  66.6 0.3 fusion.47
  67.6 0.7 fusion.9
  68.3 1.2 pad_maximum_fusion.6
  69.5 0.8 copy-done.5
  70.3 3.0 %add_select_fusion.3 = (f32[128,2048]{1,0:T(8,128)S(1)}, f32[128,2048]{1,0:T(8,128)S(1)}, f32[128,2048]{1,0:T(8,128)S(1)}, f32[128,2048]{1,0:T(8,128)S(1)}) fusion(f32[256,2048]{1,0:T(8,128)} %get-tuple-element.52, f32[256,2048]{1,0:T(8,128)S(1)} %copy-done.5, pred[128]{0:T(512)(128)(4,1)S(1)} %iota_compare_fusion, f32[256,2048]{1,0:T(8,128)} %get-tuple-element.54), kind=kLoop, calls=%fused_computation.70 | loop fusion | flops 4194304 | bytes 10485888 | tf_op jit(solution)/shard_map/jit(_where)/select_n | solution.py:68
  73.2 0.3 fusion.40
  73.9 0.3 fusion.11
  74.2 0.3 fusion.44
  74.9 0.3 fusion.10
  75.2 0.9 copy-done.8
  76.1 0.3 copy-done.9
  76.4 1.9 %fusion.17 = (bf16[256,2048]{1,0:T(8,128)(2,1)}, bf16[256,2048]{1,0:T(8,128)(2,1)}) fusion(bf16[256,2048]{1,0:T(8,128)(2,1)S(1)} %copy-done.9, f32[128,2048]{1,0:T(8,128)S(1)} %fusion.10, f32[128,2048]{1,0:T(8,128)S(1)} %fusion.11, bf16[256,2048]{1,0:T(8,128)(2,1)S(1)} %copy-done.8), kind=kLoop, calls=%fused_computation.41 | loop fusion | flops 3670016 | bytes 6291456 | tf_op jit(solution)/shard_map/convert_element_type | solution.py:123
  78.3 71.7 %all-reduce.2.cloned.1.call-done = f32[129,2048]{1,0:T(8,128)} async-done(((f32[129,2048]{1,0:T(8,128)}), f32[129,2048]{1,0:T(8,128)}) %all-reduce.2.cloned.1.call-update) | async-done | bytes 1056784 | tf_op jit(solution)/shard_map/psum | solution.py:118
  150.1 1.4 broadcast_multiply_fusion
  151.4 0.6 slice.230
  152.0 1.1 slice.229
  (43 shorter events, 2.8 us)
Async XLA Ops:
  7.2 7.9 %copy-start = (bf16[128,2048]{1,0:T(8,128)(2,1)S(1)}, bf16[128,2048]{1,0:T(8,128)(2,1)}, u32[]{:S(2)}) copy-start(bf16[128,2048]{1,0:T(8,128)(2,1)} %param.11) | copy-start | bytes 1572868
  7.2 7.0 %copy-start.13 = (bf16[256,128]{1,0:T(8,128)(2,1)S(1)}, bf16[256,128]{1,0:T(8,128)(2,1)}, u32[]{:S(2)}) copy-start(bf16[256,128]{1,0:T(8,128)(2,1)} %constant.18) | copy-start | bytes 196612
  7.2 142.9 %all-reduce.2.cloned.1.call-start = ((), (), s32[]{:S(2)}) async-start(), calls=%async_computation | async-start | bytes 2228224 | tf_op jit(solution)/shard_map/psum | solution.py:118
  9.3 16.0 %collective-permute-start = (bf16[128,2048]{1,0:T(8,128)(2,1)S(1)}, bf16[128,2048]{1,0:T(8,128)(2,1)S(1)}, u32[]{:S(2)}, u32[]{:S(2)}) collective-permute-start(bf16[128,2048]{1,0:T(8,128)(2,1)S(1)} %slice.194), channel_id=1, source_target_pairs={{0,4},{4,8},{8,12},{12,16},{16,20},{20,24},{24,28},{1,5},{5,9},{9,... | collective-permute-start | bytes 1572872 | tf_op jit(solution)/shard_map/ppermute | solution.py:16
  14.6 0.9 copy-start.12
  15.9 11.7 %copy-start.4 = (f32[256,2048]{1,0:T(8,128)}, f32[256,2048]{1,0:T(8,128)S(1)}, u32[]{:S(2)}) copy-start(f32[256,2048]{1,0:T(8,128)S(1)} %convolution_add_fusion.6) | copy-start | bytes 6291460
  27.6 1.4 copy-start.2
  27.7 1.4 copy-start.7
  29.1 0.8 copy-start.14
  31.2 1.3 copy-start.10
  31.2 1.9 %copy-start.11 = (bf16[256,2048]{1,0:T(8,128)(2,1)S(1)}, bf16[256,2048]{1,0:T(8,128)(2,1)}, u32[]{:S(2)}) copy-start(bf16[256,2048]{1,0:T(8,128)(2,1)} %param.13) | copy-start | bytes 3145732
  31.2 1.9 %copy-start.15 = (f32[2048]{0:T(1024)S(1)}, f32[2048]{0:T(1024)}, u32[]{:S(2)}) copy-start(f32[2048]{0:T(1024)} %param.12) | copy-start | bytes 24580
  31.6 1.0 copy-start.6
  44.1 16.3 %collective-permute-start.1 = (bf16[128,2048]{1,0:T(8,128)(2,1)S(1)}, bf16[128,2048]{1,0:T(8,128)(2,1)S(1)}, u32[]{:S(2)}, u32[]{:S(2)}) collective-permute-start(bf16[128,2048]{1,0:T(8,128)(2,1)S(1)} %slice.211), channel_id=1, source_target_pairs={{4,0},{8,4},{12,8},{16,12},{20,16},{24,20},{28,24},{5,1},{9,5},{13... | collective-permute-start | bytes 1572872 | tf_op jit(solution)/shard_map/ppermute | solution.py:16
  63.5 1.9 %copy-start.3 = (f32[256,2048]{1,0:T(8,128)S(1)}, f32[256,2048]{1,0:T(8,128)}, u32[]{:S(2)}) copy-start(f32[256,2048]{1,0:T(8,128)} %copy-done.2) | copy-start | bytes 6291460
  68.3 2.0 %copy-start.5 = (f32[256,2048]{1,0:T(8,128)S(1)}, f32[256,2048]{1,0:T(8,128)}, u32[]{:S(2)}) copy-start(f32[256,2048]{1,0:T(8,128)} %copy-done.4) | copy-start | bytes 6291460
  74.9 1.2 copy-start.8
  74.9 1.5 copy-start.9
  76.4 76.7 %copy-start.1 = (bf16[128,2048]{1,0:T(8,128)(2,1)S(1)}, bf16[128,2048]{1,0:T(8,128)(2,1)}, u32[]{:S(2)}) copy-start(bf16[128,2048]{1,0:T(8,128)(2,1)} %param.11) | copy-start | bytes 1572868
Sparse Core Ops, SparseCore 0:
  69.6 80.3 all-reduce.1
where the time goes:
time: 160 us
  waiting for transfers between devices  95.1 us (59%)
  other arithmetic  17.8 us (11%)
  between operations  14.5 us (9%)
  matrix products  14.1 us (9%)
  starting transfers between devices  6.41 us (4%)
  local copies, waits for them, and re-layouts  6.36 us (4%)
  blocking collectives  5.71 us (4%)
    psum x1, waiting for transfers between devices, on_device(): lax.psum(jnp.concatenate([filter_local, gain_local[None]], 0), 'ctx')  71.7 us
    ppermute x2, waiting for transfers between devices, passed_along(): return lax.ppermute(array, axis, pairs)  23.3 us
    dot_general x14, matrix products, to_spec(): jnp.dot(forward, jnp.concatenate([rows, rows], 0), preferred_element_type...  8.98 us
    ppermute x2, starting transfers between devices, passed_along(): return lax.ppermute(array, axis, pairs)  6.38 us
    psum x1, blocking collectives, on_device(): lax.psum(jnp.stack([jnp.sum(gated * gated, 1), jnp.sum(grad_scaled * gate...  5.71 us
    dot_general x15, matrix products, from_spec(): jnp.dot(back, jnp.concatenate([high, high, low], 0), preferred_element_ty...  5.13 us
    unnamed x32, local copies, waits for them, and re-layouts  4.61 us
    convert_element_type x1, other arithmetic, on_device(): grad_conv = (grad_gated * query_wide).astype(BF16)  4.54 us
  transfers between devices with their start and end apart: 3, of which 3 were waited for; matrix products, arithmetic and copies ran while one was open for 6% of the time, Pallas kernels for 0%

commit v1 on v0

--- a/solution.py
+++ b/solution.py
@@ -8,6 +8,12 @@
 EPS = 1e-06
 F32 = jnp.float32
 BF16 = jnp.bfloat16
+
+
+def gather_and_add(x, name):
+    parts = lax.all_gather(x, name, axis=0, tiled=False)
+    summed = parts.sum(axis=0)
+    return summed
 
 
 def passed_along(array, axis, by):
@@ -115,7 +121,7 @@
     filter_spec = sum((product(gc_spec[b], kv_win[b], True) for b in range(blocks)))
     filter_local = from_spec(filter_spec)
     gain_local = jnp.sum(grad_wide * normed, 0)
-    total = lax.psum(jnp.concatenate([filter_local, gain_local[None]], 0), "ctx") * scale
+    total = gather_and_add(jnp.concatenate([filter_local, gain_local[None]], 0), "ctx") * scale
     gc_spec = gc_spec + [to_spec(after)]
     gc_win = [gc_spec[b] + flip(gc_spec[b + 1]) for b in range(blocks)]
     grad_kv = jnp.concatenate([from_spec(product(w, filt, True)) for w in gc_win], 0)

time: 160 us -> 216 us (1.35)
  waiting for transfers between devices: 95.1 us -> 148 us
  other arithmetic: 17.8 us -> 21 us
    all_gather x0 -> x1, waiting for transfers between devices: none -> 124 us  [gather_and_add(): parts = lax.all_gather(x, name, axis=0, tiled=False)]
    psum x1 -> x0, waiting for transfers between devices: 71.7 us -> none  [on_device(): lax.psum(jnp.concatenate([filter_local, gain_local[None]], 0), 'ctx')]
    reduce_sum x0 -> x1, other arithmetic: none -> 4.55 us  [gather_and_add(): summed = parts.sum(axis=0)]
  transfers between devices with their start and end apart: 3 -> 3, of which waited for: 3 -> 3; matrix products, arithmetic and copies ran while one was open for 6% -> 4% of each run, Pallas kernels for 0% -> 0%
where the time goes in v1:
time: 216 us
  waiting for transfers between devices  148 us (69%)
  other arithmetic  21 us (10%)
  between operations  14.4 us (7%)
  matrix products  14.2 us (7%)
  local copies, waits for them, and re-layouts  6.45 us (3%)
  starting transfers between devices  6.41 us (3%)
  blocking collectives  5.71 us (3%)
    all_gather x1, waiting for transfers between devices, gather_and_add(): parts = lax.all_gather(x, name, axis=0, tiled=False)  124 us
    ppermute x2, waiting for transfers between devices, passed_along(): return lax.ppermute(array, axis, pairs)  23.3 us
    dot_general x14, matrix products, to_spec(): jnp.dot(forward, jnp.concatenate([rows, rows], 0), preferred_element_type...  9.04 us
    ppermute x2, starting transfers between devices, passed_along(): return lax.ppermute(array, axis, pairs)  6.38 us
    psum x1, blocking collectives, on_device(): lax.psum(jnp.stack([jnp.sum(gated * gated, 1), jnp.sum(grad_scaled * gate...  5.71 us
    dot_general x15, matrix products, from_spec(): jnp.dot(back, jnp.concatenate([high, high, low], 0), preferred_element_ty...  5.15 us
    unnamed x32, local copies, waits for them, and re-layouts  4.7 us
    reduce_sum x1, other arithmetic, gather_and_add(): summed = parts.sum(axis=0)  4.55 us
  transfers between devices with their start and end apart: 3, of which 3 were waited for; matrix products, arithmetic and copies ran while one was open for 4% of the time, Pallas kernels for 0%

profile of v1, /device:TPU:0, one launch (start us, length us, event | category | flops | bytes accessed | tf_op | source)
XLA Modules:
  0.0 215.9 jit_solution(8109991458813567092)
XLA Ops:
  7.2 2.0 fusion.18
  9.3 4.9 %collective-permute-start = (bf16[128,2048]{1,0:T(8,128)(2,1)S(1)}, bf16[128,2048]{1,0:T(8,128)(2,1)S(1)}, u32[]{:S(2)}, u32[]{:S(2)}) collective-permute-start(bf16[128,2048]{1,0:T(8,128)(2,1)S(1)} %slice.194), channel_id=1, source_target_pairs={{0,4},{4,8},{8,12},{12,16},{16,20},{20,24},{24,28},{1,5},{5,9},{9,... | collective-permute-start | bytes 1572872 | tf_op jit(solution)/shard_map/ppermute | solution.py:22
  14.2 0.4 fusion.67
  14.6 0.4 fusion.29
  15.1 0.4 fusion.74
  15.5 0.4 convolution_add_fusion.6
  16.0 9.4 %collective-permute-done = bf16[128,2048]{1,0:T(8,128)(2,1)S(1)} collective-permute-done((bf16[128,2048]{1,0:T(8,128)(2,1)S(1)}, bf16[128,2048]{1,0:T(8,128)(2,1)S(1)}, u32[]{:S(2)}, u32[]{:S(2)}) %collective-permute-start) | collective-permute-done | bytes 524320 | tf_op jit(solution)/shard_map/ppermute | solution.py:22
  25.3 0.4 fusion.75
  25.7 0.4 fusion.5
  26.3 0.7 maximum_add_fusion
  27.2 0.5 fusion.4
  27.7 1.0 subtract_select_fusion.1
  28.6 0.4 copy-done.2
  29.1 0.3 fusion.32
  29.4 0.5 copy-done.14
  29.9 0.3 convolution_add_fusion.16
  31.3 0.3 fusion.12
  31.6 1.0 copy-done.6
  32.6 0.6 copy-done.11
  33.1 0.7 multiply_reduce_fusion
  33.8 5.7 %psum.7 = f32[2,256]{1,0:T(2,128)S(1)} all-reduce(f32[2,256]{1,0:T(2,128)S(1)} %pad_maximum_fusion.6), channel_id=1, replica_groups=mesh['ctx'=8,'tp'=4] {'tp'}, use_global_device_ids=true, to_apply=%region_2.3 | all-reduce | flops 512 | bytes 4096 | tf_op jit(solution)/shard_map/psum | solution.py:111
  39.6 4.5 %fusion.16 = (bf16[256,2048]{1,0:T(8,128)(2,1)S(1)}, bf16[256,2048]{1,0:T(8,128)(2,1)}, f32[2048]{0:T(1024)S(1)}, bf16[256,2048]{1,0:T(8,128)(2,1)}) fusion(bf16[256,2048]{1,0:T(8,128)(2,1)} %param.8, f32[256]{0:T(256)S(1)} %multiply_multiply_fusion, f32[256]{0:T(256)S(1)} %bitcast.71, f32[2048]{0:T(1024)S(1)} %copy-done.15, bf16[256,2048]{1,0:T(8,128)(2,1)} %param.13, ...), kind=kLoop, calls=%fused_computation.40 | loop fusion | flops 8910848 | bytes 7358464 | tf_op jit(solution)/shard_map/convert_element_type | solution.py:118
  44.1 1.5 collective-permute-start.1
  45.6 0.4 fusion.64
  46.1 0.4 fusion.26
  46.5 14.0 %collective-permute-done.1 = bf16[128,2048]{1,0:T(8,128)(2,1)S(1)} collective-permute-done((bf16[128,2048]{1,0:T(8,128)(2,1)S(1)}, bf16[128,2048]{1,0:T(8,128)(2,1)S(1)}, u32[]{:S(2)}, u32[]{:S(2)}) %collective-permute-start.1) | collective-permute-done | bytes 524320 | tf_op jit(solution)/shard_map/ppermute | solution.py:22
  60.4 0.4 fusion.76
  60.9 0.4 fusion
  61.5 1.9 maximum_add_fusion.2
  63.6 1.8 maximum_add_fusion.1
  65.4 1.2 add_select_fusion.1
  66.7 0.3 fusion.47
  67.6 0.7 fusion.9
  68.4 1.1 maximum_bitcast_fusion
  69.5 0.9 copy-done.5
  70.3 3.0 %add_select_fusion.3 = (f32[128,2048]{1,0:T(8,128)S(1)}, f32[128,2048]{1,0:T(8,128)S(1)}, f32[128,2048]{1,0:T(8,128)S(1)}, f32[128,2048]{1,0:T(8,128)S(1)}) fusion(f32[256,2048]{1,0:T(8,128)} %get-tuple-element.52, f32[256,2048]{1,0:T(8,128)S(1)} %copy-done.5, pred[128]{0:T(512)(128)(4,1)S(1)} %iota_compare_fusion, f32[256,2048]{1,0:T(8,128)} %get-tuple-element.54), kind=kLoop, calls=%fused_computation.70 | loop fusion | flops 4194304 | bytes 10485888 | tf_op jit(solution)/shard_map/jit(_where)/select_n | solution.py:74
  73.6 0.3 fusion.44
  74.0 0.3 convolution_add_fusion.12
  74.3 0.3 fusion.11
  74.6 0.3 convolution_add_fusion.10
  75.0 0.3 fusion.10
  75.3 0.9 copy-done.8
  76.2 0.3 copy-done.9
  76.5 1.9 fusion.17
  78.4 124.3 %all-gather.4.cloned.1.call-done = f32[8,129,2048]{2,1,0:T(8,128)} async-done(((f32[1,129,2048]{2,1,0:T(8,128)}), f32[8,129,2048]{2,1,0:T(8,128)}) %all-gather.4.cloned.1.call-update) | async-done | bytes 8454160 | tf_op jit(solution)/shard_map/all_gather | solution.py:14
  202.7 4.5 %reduce_sum.39 = f32[129,2048]{1,0:T(8,128)S(1)} reduce(f32[8,129,2048]{2,1,0:T(8,128)} %all-gather.4.cloned.1.call-done, f32[]{:T(128)} %constant.5.clone.1), dimensions={0}, to_apply=%region_4.5 | reduce | flops 1849344 | bytes 9510916 | tf_op jit(solution)/shard_map/reduce_sum | solution.py:15
  207.4 0.6 slice.230
  208.0 1.1 slice.229
  (44 shorter events, 3.0 us)
Async XLA Ops:
  7.2 7.9 %copy-start = (bf16[128,2048]{1,0:T(8,128)(2,1)S(1)}, bf16[128,2048]{1,0:T(8,128)(2,1)}, u32[]{:S(2)}) copy-start(bf16[128,2048]{1,0:T(8,128)(2,1)} %param.11) | copy-start | bytes 1572868
  7.2 7.0 %copy-start.13 = (bf16[256,128]{1,0:T(8,128)(2,1)S(1)}, bf16[256,128]{1,0:T(8,128)(2,1)}, u32[]{:S(2)}) copy-start(bf16[256,128]{1,0:T(8,128)(2,1)} %constant.18) | copy-start | bytes 196612
  7.2 195.5 %all-gather.4.cloned.1.call-start = ((), (), s32[]{:S(2)}) async-start(), calls=%async_computation | async-start | bytes 10027008 | tf_op jit(solution)/shard_map/all_gather | solution.py:14
  9.3 16.0 %collective-permute-start = (bf16[128,2048]{1,0:T(8,128)(2,1)S(1)}, bf16[128,2048]{1,0:T(8,128)(2,1)S(1)}, u32[]{:S(2)}, u32[]{:S(2)}) collective-permute-start(bf16[128,2048]{1,0:T(8,128)(2,1)S(1)} %slice.194), channel_id=1, source_target_pairs={{0,4},{4,8},{8,12},{12,16},{16,20},{20,24},{24,28},{1,5},{5,9},{9,... | collective-permute-start | bytes 1572872 | tf_op jit(solution)/shard_map/ppermute | solution.py:22
  14.6 0.9 copy-start.12
  15.9 11.7 %copy-start.4 = (f32[256,2048]{1,0:T(8,128)}, f32[256,2048]{1,0:T(8,128)S(1)}, u32[]{:S(2)}) copy-start(f32[256,2048]{1,0:T(8,128)S(1)} %convolution_add_fusion.6) | copy-start | bytes 6291460
  27.6 1.4 copy-start.2
  27.7 1.4 copy-start.7
  29.1 0.8 copy-start.14
  31.2 1.3 copy-start.10
  31.2 1.9 copy-start.11
  31.2 1.9 copy-start.15
  31.6 1.0 copy-start.6
  44.1 16.3 %collective-permute-start.1 = (bf16[128,2048]{1,0:T(8,128)(2,1)S(1)}, bf16[128,2048]{1,0:T(8,128)(2,1)S(1)}, u32[]{:S(2)}, u32[]{:S(2)}) collective-permute-start(bf16[128,2048]{1,0:T(8,128)(2,1)S(1)} %slice.211), channel_id=1, source_target_pairs={{4,0},{8,4},{12,8},{16,12},{20,16},{24,20},{28,24},{5,1},{9,5},{13... | collective-permute-start | bytes 1572872 | tf_op jit(solution)/shard_map/ppermute | solution.py:22
  63.6 1.9 copy-start.3
  68.3 2.0 copy-start.5
  74.9 1.2 copy-start.8
  75.0 1.5 copy-start.9
  202.7 6.3 %copy-start.1 = (bf16[128,2048]{1,0:T(8,128)(2,1)S(1)}, bf16[128,2048]{1,0:T(8,128)(2,1)}, u32[]{:S(2)}) copy-start(bf16[128,2048]{1,0:T(8,128)(2,1)} %param.11) | copy-start | bytes 1572868
Sparse Core Ops, SparseCore 0:
  69.6 133.0 all-gather.3
